TPU v7x, 256 devices: a whole 4x4x8 slice. The times are simulated.
256 devices in a mesh: dp: 8 (over x, core), proto: 32 (over z, y).
Axes of the slice: x: 4, y: 4, z: 8, core: 2. Of those that a mesh axis runs over, the one named last changes fastest.
Arguments:
- student_feats: bfloat16 [5120, 256], P(('dp', 'proto')), may hold values from -20 to 20
- teacher_feats: bfloat16 [1024, 256], P(('dp', 'proto')), may hold values from -20 to 20
- prototypes: bfloat16 [256, 65536], P(None, 'proto'), may hold values from -80 to 80
- teacher_prototypes: bfloat16 [256, 65536], P(None, 'proto'), may hold values from -80 to 80
- crop_image: int32 [5120], P('dp'), may hold values from 0 to 511, as said below
- pairing: int32 [5120, 2], P('dp'), may hold values 0 or 1
Outputs:
- student_grad: float32 [5120, 256], P(('dp', 'proto'))
- prototype_grad: float32 [256, 65536], P('dp', 'proto')
Inputs may be any that keep to these rules, and one draw needn't show every extreme that they name: `crop_image`: rows j * 64 * 10 to (j + 1) * 64 * 10 - 1 name only images j * 64 to (j + 1) * 64 - 1, each of them exactly 10 times.
All inputs are finite; a program needn't handle non-finite values. No bound on the sum of `pairing` on one device may be relied on, other than what follows from the above.
Results may differ from a plain program's by a relative error of at most 0.012.
The roundings to bfloat16 on the way count: a program that leaves them out, or rounds other values in their place, can miss the bound.
Values may be sent and summed in bfloat16 or wider, within the bound.
A program may use at most 64 MiB of HBM per device.

v0:
```python
import jax
import jax.numpy as jnp
from jax import lax
from jax.experimental import pallas as pl
from jax.experimental.pallas import tpu as pltpu
from jax.sharding import PartitionSpec as P

MESH = pl.DeviceIdType.MESH
F32 = jnp.float32
BF16 = jnp.bfloat16

IMG_DEV = 64
EPS = 1e-06
TEACHER_SCALE = 1.0 / 0.07
STUDENT_SCALE = 1.0 / 0.1
GRAD_SCALE = 4096.0 / 0.1

NDP = 8
NPR = 32
K = 256
C = 2048
R = 640
T = 128
OWN = 20
PAD = 48
HPAD = 24
CH = 512

(
    X_TEACH, X_STUDZ, X_STUDY, X_COL1, X_TGRP, X_ROW1, X_COL2, X_TOT, X_ROW2, X_HY0, X_HY1, X_HZ0, X_HZ1, X_UT, X_ROW3, X_G, X_PG, X_GALL, X_DOT
) = range(19)
N_X = 19
SIZES = {"dp": 8, "proto": 32, "z": 8, "y": 4}


def row_to_columns(row):
    return jnp.transpose(jnp.broadcast_to(row, (128, 128)))


def columns_to_row(part):
    return jnp.sum(jnp.transpose(part), axis=0, keepdims=True)


def lane_tiles(value):
    total = value[:, 0:128]
    for j in range(1, value.shape[1] // 128):
        total = total + value[:, 128 * j : 128 * j + 128]
    return total


def dot(a, b):
    return jnp.dot(a, b, preferred_element_type=F32)


def dot_nt(a, b):
    return lax.dot_general(a, b, (((1,), (1,)), ((), ())), preferred_element_type=F32)


def kernel(
    sfh, tfh, prh, tph, croph, pairh,
    sgrad, pgrad,
    teach, stud, col1, tgrp, row1, col2, tot, row2, hybuf, hzbuf, utbuf, row3, gbuf, pgbuf, gall, dotbuf,
    hsend, hzsend, utsend, gsend, pgsend,
    pack, x32, xb, xt, wb, tpb, pnorm, pown, expo, expb, probb, selb, scalec, harr, garr, ass, assb, mown, cvec, avec,
    sdir, snorm, ownsel, sf, tf, pr, tp, crop, pair,
    ssem, rsem, lsem,
):
    dp = lax.axis_index("dp")
    pi = lax.axis_index("proto")

    pz, py = pi // 4, lax.rem(pi, 4)

    def far_first(i, half):
        return half + ((i + 1) // 2) * (1 - 2 * lax.rem(i, 2))

    def peer(axis, i):
        if axis == "dp":
            return lax.rem(dp + i + 1, NDP)
        if axis == "z":
            return lax.rem(pz + far_first(i, 4), 8)
        if axis == "y":
            return lax.rem(py + far_first(i, 2), 4)
        return lax.rem(pz + far_first(i // 4, 4), 8) * 4 + lax.rem(py + far_first(lax.rem(i, 4), 2), 4)

    def address(axis, p):
        if axis == "dp":
            return (p, pi)
        if axis == "z":
            return (dp, p * 4 + py)
        if axis == "y":
            return (dp, pz * 4 + p)
        return (dp, p)

    def mine(axis):
        return {"dp": dp, "proto": pi, "z": pz, "y": py}[axis]

    def count(axis):
        return SIZES[axis]

    def send(x, axis, dst, src=None):
        me = mine(axis)

        @pl.loop(0, count(axis) - 1)
        def _(i):
            p = peer(axis, i)
            pltpu.make_async_remote_copy(
                src_ref=dst.at[me] if src is None else src.at[p],
                dst_ref=dst.at[me],
                send_sem=ssem.at[x],
                recv_sem=rsem.at[x],
                device_id=address(axis, p),
                device_id_type=MESH,
            ).start()

    def arrived(x, axis, dst):
        blocks = dst.at[pl.ds(0, count(axis) - 1)]
        pltpu.make_async_copy(blocks, blocks, rsem.at[x]).wait()

    def sent(x, axis, dst):
        blocks = dst.at[pl.ds(0, count(axis) - 1)]
        pltpu.make_async_copy(blocks, blocks, ssem.at[x]).wait()

    def group_rows(g):
        return pl.ds(pl.multiple_of(g * T, T), T)

    barrier = pltpu.get_barrier_semaphore()
    for axis in ("proto", "dp"):
        @pl.loop(0, count(axis) - 1)
        def _(i, axis=axis):
            p = peer(axis, i)
            pl.semaphore_signal(barrier, inc=1, device_id=address(axis, p), device_id_type=MESH)

    loads = []
    for k, (src, dst) in enumerate(
        ((tfh, tf), (sfh, sf), (tph, tp), (prh, pr), (croph, crop), (pairh, pair))
    ):
        loads.append(pltpu.make_async_copy(src, dst, lsem.at[k]))
        loads[-1].start()

    loads[0].wait()
    tw = tf[...].astype(F32)
    tu = tw / jnp.sqrt(jnp.sum(tw * tw, axis=1, keepdims=True) + EPS)
    teach[pi, 0:4, :] = tu[:, 0:128].astype(BF16).astype(F32)
    teach[pi, 4:8, :] = tu[:, 128:256].astype(BF16).astype(F32)
    loads[1].wait()
    sw = sf[...].astype(F32)
    sn = jnp.sqrt(jnp.sum(sw * sw, axis=1, keepdims=True) + EPS)
    sd = sw / sn
    snorm[...] = jnp.broadcast_to(sn, (OWN, 128))
    sdir[...] = sd
    pack[...] = jnp.zeros_like(pack)
    hsend[...] = jnp.zeros_like(hsend)
    pack[0:OWN, :] = sd[:, 0:128]
    pack[24 : 24 + OWN, :] = sd[:, 128:256]
    stud[py, pz] = pack[...].astype(BF16)

    loads[2].wait()

    @pl.loop(0, C // 256)
    def _(j):
        cols = pl.ds(pl.multiple_of(j * 256, 256), 256)
        v = tp[:, cols].astype(F32)
        inv = 1.0 / jnp.sqrt(jnp.sum(v * v, axis=0, keepdims=True) + EPS)
        tpb[:, cols] = (v * inv).astype(BF16)

    pl.semaphore_wait(barrier, NPR - 1 + NDP - 1)
    send(X_TEACH, "proto", teach)
    send(X_STUDZ, "z", stud.at[py])

    loads[3].wait()

    @pl.loop(0, C // 256)
    def _(j):
        cols = pl.ds(pl.multiple_of(j * 256, 256), 256)
        v = pr[:, cols].astype(F32)
        n = jnp.sqrt(jnp.sum(v * v, axis=0, keepdims=True) + EPS)
        pnorm[:, cols] = n
        wb[:, cols] = (v * (1.0 / n)).astype(BF16)

    loads[4].wait()
    loads[5].wait()
    lanes = lax.broadcasted_iota(jnp.int32, (128, 128), 1).astype(F32)
    base = (dp * IMG_DEV).astype(F32)
    for i in range(R // 128):
        image = row_to_columns(crop[i : i + 1, :].astype(F32)) - base
        w0 = row_to_columns(pair[0:1, 128 * i : 128 * i + 128].astype(F32))
        w1 = row_to_columns(pair[1:2, 128 * i : 128 * i + 128].astype(F32))
        sel = jnp.where(lanes == 2.0 * image, w0, 0.0) + jnp.where(lanes == 2.0 * image + 1.0, w1, 0.0)
        selb[128 * i : 128 * i + 128, :] = sel.astype(BF16)
        scalec[128 * i : 128 * i + 128, :] = w0 + w1
    own_rows = lax.broadcasted_iota(jnp.int32, (32, R), 0) + pi * OWN
    ownsel[...] = (lax.broadcasted_iota(jnp.int32, (32, R), 1) == own_rows).astype(F32)

    arrived(X_TEACH, "proto", teach)
    for p in range(NPR):
        v = teach[p]
        x32[4 * p : 4 * p + 4, 0:128] = v[0:4]
        x32[4 * p : 4 * p + 4, 128:256] = v[4:8]
    tgrp[dp] = x32[0:T, :].astype(BF16)

    def assign(g):
        rows = tgrp[g]
        for j in range(C // CH):
            e = jnp.exp(dot(rows, tpb[:, CH * j : CH * j + CH]) * TEACHER_SCALE)
            ass[group_rows(g), CH * j : CH * j + CH] = e

    assign(dp)

    def column_part(g, acc, arow, table=ass):
        if arow is not None:
            wide = row_to_columns(arow)
        for i in range(T // 8):
            e = table[pl.ds(pl.multiple_of(g * T + 8 * i, 8), 8), :]
            if arow is not None:
                e = e * jnp.concatenate([wide[8 * i : 8 * i + 8]] * (C // 128), axis=1)
            acc = acc + e
        return acc

    def row_part(g):
        cb = jnp.broadcast_to(cvec[...], (8, C))
        parts = []
        for i in range(T // 8):
            parts.append(lane_tiles(ass[pl.ds(pl.multiple_of(g * T + 8 * i, 8), 8), :] * cb))
        return columns_to_row(jnp.concatenate(parts, axis=0))

    col1[dp] = jnp.sum(column_part(dp, jnp.zeros((8, C), F32), None), axis=0, keepdims=True)
    send(X_COL1, "dp", col1)
    send(X_TGRP, "dp", tgrp)
    arrived(X_STUDZ, "z", stud.at[py])
    send(X_STUDY, "y", stud)

    arrived(X_COL1, "dp", col1)
    cvec[...] = 1.0 / jnp.sum(col1[...], axis=0)
    row1[pi] = row_part(dp)
    send(X_ROW1, "proto", row1)

    arrived(X_STUDY, "y", stud)
    for p in range(NPR):
        v = stud[p % 4, p // 4].astype(F32)
        x32[OWN * p : OWN * p + OWN, 0:128] = v[0:OWN]
        x32[OWN * p : OWN * p + OWN, 128:256] = v[24 : 24 + OWN]
    xb[...] = x32[...].astype(BF16)
    for i in range(R // 128):
        xt[:, 128 * i : 128 * i + 128] = jnp.transpose(x32[128 * i : 128 * i + 128, :]).astype(BF16)

    @pl.loop(0, R // 128)
    def _(i):
        rows = pl.ds(pl.multiple_of(i * 128, 128), 128)
        part = jnp.zeros((128, 128), F32)
        for j in range(C // CH):
            e = jnp.exp(dot(xb[rows, :], wb[:, CH * j : CH * j + CH]) * STUDENT_SCALE)
            expo[rows, CH * j : CH * j + CH] = e
            expb[rows, CH * j : CH * j + CH] = e.astype(BF16)
            part = part + lane_tiles(e)
        tot[pi, pl.ds(i, 1), :] = columns_to_row(part)

    tot[pi, 5:8, :] = jnp.ones((3, 128), F32)

    @pl.loop(0, R // 128)
    def _(i):
        rows = pl.ds(pl.multiple_of(i * 128, 128), 128)
        harr[rows, :] = dot_nt(expb[rows, :], wb[...])

    for p in range(NPR):
        for half in range(2):
            hsend[half, p % 4, p // 4, 0:OWN, :] = harr[OWN * p : OWN * p + OWN, 128 * half : 128 * half + 128]
    for half in range(2):
        hybuf[half, py] = hsend[half, py]

    arrived(X_ROW1, "proto", row1)
    avec[0:1, :] = 1.0 / jnp.sum(row1[...], axis=0)
    col2[dp] = jnp.sum(column_part(dp, jnp.zeros((8, C), F32), avec[0:1, :]), axis=0, keepdims=True)
    send(X_COL2, "dp", col2)
    send(X_HY0, "y", hybuf.at[0], hsend.at[0])
    send(X_TOT, "proto", tot)

    def half_sums(half, x, y):
        arrived(x, "y", hybuf.at[half])
        for z in range(8):
            hzsend[half, z] = jnp.sum(hybuf[half, :, z], axis=0)
        send(y, "z", hzbuf.at[half], hzsend.at[half])
        hzbuf[half, pz] = hzsend[half, pz]

    arrived(X_TGRP, "dp", tgrp)

    @pl.loop(1, NDP)
    def _(i):
        assign(lax.rem(dp + i, NDP))

    def columns():
        acc = lax.fori_loop(
            0, NDP, lambda g, acc: column_part(g, acc, avec[pl.ds(g, 1), :]), jnp.zeros((8, C), F32)
        )
        cvec[...] = 1.0 / jnp.sum(acc, axis=0, keepdims=True)

    def rows_into(buf):
        @pl.loop(0, NDP)
        def _(g):
            buf[pi, pl.ds(g, 1), :] = row_part(g)

    arrived(X_COL2, "dp", col2)
    cvec[...] = 1.0 / jnp.sum(col2[...], axis=0)
    rows_into(row2)
    send(X_ROW2, "proto", row2)
    send(X_HY1, "y", hybuf.at[1], hsend.at[1])

    half_sums(0, X_HY0, X_HZ0)

    ut = dot(xt[...], selb[...])
    for g in range(NDP):
        utsend[g] = ut[32 * g : 32 * g + 32, :]
    send(X_UT, "dp", utbuf, utsend)
    utbuf[dp] = utsend[dp]

    arrived(X_TOT, "proto", tot)
    inv_tot = 1.0 / jnp.sum(tot[...], axis=0)
    for i in range(R // 128):
        rows = slice(128 * i, 128 * i + 128)
        scalec[rows, :] = scalec[rows, :] * row_to_columns(inv_tot[i : i + 1, :])

    @pl.loop(0, R // 16)
    def _(i):
        rows = pl.ds(pl.multiple_of(i * 16, 16), 16)
        s = scalec[rows, :]
        probb[rows, :] = (expo[rows, :] * jnp.concatenate([s] * (C // 128), axis=1)).astype(BF16)

    for j in range(C // CH):
        cols = slice(CH * j, CH * j + CH)
        pg = dot(xt[...], probb[:, cols])
        direction = pr[:, cols].astype(F32) / pnorm[:, cols]
        pg = (pg - direction * jnp.sum(direction * pg, axis=0, keepdims=True)).astype(BF16)
        for g in range(NDP):
            pgsend[g, :, cols] = pg[32 * g : 32 * g + 32, :]
    send(X_PG, "dp", pgbuf, pgsend)
    pgbuf[dp] = pgsend[dp]

    ur = jnp.transpose(ut)
    utb = ur.astype(BF16)
    utb = jnp.concatenate([utb, (ur - utb.astype(F32)).astype(BF16)], axis=0)
    for j in range(C // CH):
        cols = slice(CH * j, CH * j + CH)
        along = dot(utb, wb[:, cols])
        along = along[0:T] + along[T : 2 * T]
        mown[:, cols] = along * ass[group_rows(dp), cols].astype(BF16).astype(F32)

    arrived(X_ROW2, "proto", row2)
    avec[...] = 1.0 / jnp.sum(row2[...], axis=0)
    columns()

    cb = jnp.broadcast_to(cvec[...], (16, C))
    for i in range(T // 16):
        rows = pl.ds(pl.multiple_of(dp * T + 16 * i, 16), 16)
        probb[16 * i : 16 * i + 16, :] = (ass[rows, :] * cb).astype(BF16)
    garr[...] = dot_nt(probb[0:T, :], wb[...])
    for p in range(16):
        gsend[p] = garr[8 * p : 8 * p + 8, 0:128]
        gsend[p + 16] = garr[8 * p : 8 * p + 8, 128:256]
    send(X_G, "proto", gbuf, gsend)
    half_sums(1, X_HY1, X_HZ1)
    gbuf[pi] = gsend[pi]
    rows_into(row3)
    send(X_ROW3, "proto", row3)


    arrived(X_HZ0, "z", hzbuf.at[0])
    arrived(X_HZ1, "z", hzbuf.at[1])
    hsum = jnp.sum(hzbuf[...], axis=1)
    own_scale = jnp.dot(ownsel[...], scalec[...], precision=lax.Precision.HIGHEST, preferred_element_type=F32)[0:OWN, 0:1]
    own_pick = dot(ownsel[...].astype(BF16), selb[...])[0:OWN, :]

    @pl.loop(0, NDP * T // 32)
    def _(i):
        rows = pl.ds(pl.multiple_of(i * 32, 32), 32)
        assb[rows, :] = ass[rows, :].astype(BF16)

    arrived(X_G, "proto", gbuf)
    gall[pi] = jnp.sum(gbuf[...], axis=0)
    send(X_GALL, "proto", gall)

    arrived(X_ROW3, "proto", row3)
    avec[...] = 1.0 / jnp.sum(row3[...], axis=0)
    along = jnp.sum(column_part(0, jnp.zeros((8, C), F32), avec[pl.ds(dp, 1), :], mown), axis=0, keepdims=True)
    dotbuf[dp] = along * cvec[...]
    send(X_DOT, "dp", dotbuf)
    arrived(X_UT, "dp", utbuf)
    lhs = jnp.concatenate([utbuf[g] * avec[g : g + 1, :] for g in range(NDP)], axis=1)
    high = lhs.astype(BF16)
    lhs = jnp.concatenate([high, (lhs - high.astype(F32)).astype(BF16)], axis=0)
    arrived(X_PG, "dp", pgbuf)
    own32 = pl.ds(pl.multiple_of(dp * 32, 32), 32)
    for j in range(C // CH):
        cols = slice(CH * j, CH * j + CH)
        both = dot(lhs, assb[:, cols])
        target = (both[0:32] + both[32:64]) * cvec[:, cols]
        own = GRAD_SCALE * (jnp.sum(pgbuf[:, :, cols].astype(F32), axis=0) - target)
        pown[:, cols] = own

    arrived(X_DOT, "dp", dotbuf)
    for j in range(C // CH):
        cols = slice(CH * j, CH * j + CH)
        column_dot = -GRAD_SCALE * jnp.sum(dotbuf[:, :, cols], axis=0)
        inv = 1.0 / pnorm[:, cols]
        pown[:, cols] = (pown[:, cols] - pr[own32, cols].astype(F32) * (inv * column_dot)) * inv
    store = pltpu.make_async_copy(pown, pgrad, lsem.at[6])
    store.start()

    arrived(X_GALL, "proto", gall)
    gfull = jnp.concatenate([gall[0:16].reshape(T, 128), gall[16:32].reshape(T, 128)], axis=1)
    picked = jnp.dot(
        own_pick * avec[pl.ds(dp, 1), :], gfull, precision=lax.Precision.HIGHEST, preferred_element_type=F32
    )
    h = jnp.concatenate([hsum[0, 0:OWN], hsum[1, 0:OWN]], axis=1)
    unit_grad = GRAD_SCALE * (own_scale * h - picked)
    sd = sdir[...]
    sgrad[...] = (unit_grad - sd * jnp.sum(sd * unit_grad, axis=1, keepdims=True)) / snorm[:, 0:1]

    store.wait()
    for x, axis, buf in (
        (X_TEACH, "proto", teach), (X_STUDZ, "z", stud.at[py]), (X_STUDY, "y", stud), (X_COL1, "dp", col1),
        (X_TGRP, "dp", tgrp), (X_ROW1, "proto", row1), (X_COL2, "dp", col2), (X_TOT, "proto", tot),
        (X_ROW2, "proto", row2), (X_HY0, "y", hybuf.at[0]), (X_HY1, "y", hybuf.at[1]),
        (X_HZ0, "z", hzbuf.at[0]), (X_HZ1, "z", hzbuf.at[1]), (X_UT, "dp", utbuf), (X_ROW3, "proto", row3),
        (X_G, "proto", gbuf), (X_PG, "dp", pgbuf), (X_GALL, "proto", gall), (X_DOT, "dp", dotbuf),
    ):
        sent(x, axis, buf)


def last_step(student, proto, sgrad, pgrad):
    sgrad[...] = student[...]
    pgrad[...] = proto[...]


def per_device(student_feats, teacher_feats, prototypes, teacher_prototypes, crop_image, pairing):
    vmem = pl.BlockSpec(memory_space=pltpu.VMEM)
    anywhere = pl.BlockSpec(memory_space=pl.ANY)
    outs = (jax.ShapeDtypeStruct((OWN, K), F32), jax.ShapeDtypeStruct((K // NDP, C), F32))
    student, proto = pl.pallas_call(
        kernel,
        out_shape=outs,
        in_specs=[anywhere] * 6,
        out_specs=(vmem, anywhere),
        scratch_shapes=[
            pltpu.VMEM((NPR, 8, 128), F32),
            pltpu.VMEM((4, 8, PAD, 128), BF16),
            pltpu.VMEM((NDP, 1, C), F32),
            pltpu.VMEM((NDP, T, K), BF16),
            pltpu.VMEM((NPR, 1, 128), F32),
            pltpu.VMEM((NDP, 1, C), F32),
            pltpu.VMEM((NPR, 8, 128), F32),
            pltpu.VMEM((NPR, 8, 128), F32),
            pltpu.VMEM((2, 4, 8, HPAD, 128), F32),
            pltpu.VMEM((2, 8, HPAD, 128), F32),
            pltpu.VMEM((NDP, 32, 128), F32),
            pltpu.VMEM((NPR, 8, 128), F32),
            pltpu.VMEM((NPR, 8, 128), F32),
            pltpu.VMEM((NDP, 32, C), BF16),
            pltpu.VMEM((NPR, 8, 128), F32),
            pltpu.VMEM((NDP, 1, C), F32),
            pltpu.VMEM((2, 4, 8, HPAD, 128), F32),
            pltpu.VMEM((2, 8, HPAD, 128), F32),
            pltpu.VMEM((NDP, 32, 128), F32),
            pltpu.VMEM((NPR, 8, 128), F32),
            pltpu.VMEM((NDP, 32, C), BF16),
            pltpu.VMEM((PAD, 128), F32),
            pltpu.VMEM((R, K), F32),
            pltpu.VMEM((R, K), BF16),
            pltpu.VMEM((K, R), BF16),
            pltpu.VMEM((K, C), BF16),
            pltpu.VMEM((K, C), BF16),
            pltpu.VMEM((1, C), F32),
            pltpu.VMEM((K // NDP, C), F32),
            pltpu.VMEM((R, C), F32),
            pltpu.VMEM((R, C), BF16),
            pltpu.VMEM((R, C), BF16),
            pltpu.VMEM((R, 128), BF16),
            pltpu.VMEM((R, 128), F32),
            pltpu.VMEM((R, K), F32),
            pltpu.VMEM((T, K), F32),
            pltpu.VMEM((NDP * T, C), F32),
            pltpu.VMEM((NDP * T, C), BF16),
            pltpu.VMEM((T, C), F32),
            pltpu.VMEM((1, C), F32),
            pltpu.VMEM((8, 128), F32),
            pltpu.VMEM((OWN, K), F32),
            pltpu.VMEM((OWN, 128), F32),
            pltpu.VMEM((32, R), F32),
            pltpu.VMEM((OWN, K), BF16),
            pltpu.VMEM((4, K), BF16),
            pltpu.VMEM((K, C), BF16),
            pltpu.VMEM((K, C), BF16),
            pltpu.VMEM((R // 128, 128), jnp.int32),
            pltpu.VMEM((2, R), jnp.int32),
            pltpu.SemaphoreType.DMA((N_X,)),
            pltpu.SemaphoreType.DMA((N_X,)),
            pltpu.SemaphoreType.DMA((7,)),
        ],
        compiler_params=pltpu.CompilerParams(
            collective_id=0, has_side_effects=True, vmem_limit_bytes=56 * 2**20
        ),
    )(student_feats, teacher_feats, prototypes, teacher_prototypes, crop_image.reshape(R // 128, 128), pairing.T)
    return pl.pallas_call(
        last_step,
        out_shape=outs,
        in_specs=[vmem] * 2,
        out_specs=(vmem, vmem),
        compiler_params=pltpu.CompilerParams(vmem_limit_bytes=56 * 2**20),
    )(student, proto)


def solution(mesh):
    in_specs = (
        P(("dp", "proto"), None),
        P(("dp", "proto"), None),
        P(None, "proto"),
        P(None, "proto"),
        P("dp"),
        P("dp", None),
    )
    out_specs = (P(("dp", "proto"), None), P("dp", "proto"))
    return jax.shard_map(
        per_device, mesh=mesh, in_specs=in_specs, out_specs=out_specs, check_vma=False
    )
```

profile of v0, /device:TPU:1, one launch (start us, length us, event | category | flops | bytes accessed | tf_op | source)
XLA Modules:
  0.0 62.5 jit_solution(14091807389394863318)
XLA Ops:
  0.6 60.2 %shard_map.77 = (f32[20,256]{1,0:T(8,128)}, f32[32,2048]{1,0:T(8,128)}) custom-call(bf16[20,256]{1,0:T(8,128)(2,1)} %sfh.1, bf16[4,256]{1,0:T(4,128)(2,1)} %tfh.1, bf16[256,2048]{1,0:T(8,128)(2,1)} %prh.1, bf16[256,2048]{1,0:T(8,128)(2,1)} %tph.1, s32[5,128]{1,0:T(8,128)} %bitcast.3, s32[2,640]{1,0:T(2,128)} %bitcast.2), custom_call_target="tpu_custom_call" | custom-call | tf_op jit(solution)/shard_map/pallas_call | solution.py:437
  60.8 1.7 %shard_map.78 = (f32[20,256]{1,0:T(8,128)}, f32[32,2048]{1,0:T(8,128)}) custom-call(f32[20,256]{1,0:T(8,128)} %get-tuple-element.4.student, f32[32,2048]{1,0:T(8,128)} %get-tuple-element.5.proto), custom_call_target="tpu_custom_call" | custom-call | tf_op jit(solution)/shard_map/pallas_call | solution.py:501
where the time goes:
time: 62.7 us; the launch traced here: 62.5 us
  Pallas kernels  61.9 us (99%)
  between operations  0.64 us (1%)
    pallas_call x1, Pallas kernels, per_device(): pl.pallas_call(kernel, out_shape=outs, in_specs=[anywhere] * 6, out_specs...  60.2 us
    pallas_call x1, Pallas kernels, per_device(): pl.pallas_call(last_step, out_shape=outs, in_specs=[vmem] * 2, out_specs=...  1.69 us

commit v1 on v0

--- a/solution.py
+++ b/solution.py
@@ -288,15 +288,13 @@
         assign(lax.rem(dp + i, NDP))
 
     def columns():
-        acc = lax.fori_loop(
-            0, NDP, lambda g, acc: column_part(g, acc, avec[pl.ds(g, 1), :]), jnp.zeros((8, C), F32)
-        )
+        acc = jnp.zeros((8, C), F32)
+        for g in range(NDP):
+            acc = column_part(g, acc, avec[g : g + 1, :])
         cvec[...] = 1.0 / jnp.sum(acc, axis=0, keepdims=True)
 
     def rows_into(buf):
-        @pl.loop(0, NDP)
-        def _(g):
-            buf[pi, pl.ds(g, 1), :] = row_part(g)
+        buf[pi] = jnp.concatenate([row_part(g) for g in range(NDP)], axis=0)
 
     arrived(X_COL2, "dp", col2)
     cvec[...] = 1.0 / jnp.sum(col2[...], axis=0)

time: 62.7 us -> 61.2 us (0.976)
  Pallas kernels: 61.9 us -> 60.4 us
    pallas_call x1, Pallas kernels: 60.2 us -> 58.7 us  [per_device(): pl.pallas_call(kernel, out_shape=outs, in_specs=[anywhere] * 6, out_specs...]
where the time goes in v1:
time: 61.2 us; the launch traced here: 61.1 us
  Pallas kernels  60.4 us (99%)
  between operations  0.64 us (1%)
    pallas_call x1, Pallas kernels, per_device(): pl.pallas_call(kernel, out_shape=outs, in_specs=[anywhere] * 6, out_specs...  58.7 us
    pallas_call x1, Pallas kernels, per_device(): pl.pallas_call(last_step, out_shape=outs, in_specs=[vmem] * 2, out_specs=...  1.69 us

profile of v1, /device:TPU:1, one launch (start us, length us, event | category | flops | bytes accessed | tf_op | source)
XLA Modules:
  0.0 61.1 jit_solution(5952998632872603927)
XLA Ops:
  0.6 58.7 %shard_map.77 = (f32[20,256]{1,0:T(8,128)}, f32[32,2048]{1,0:T(8,128)}) custom-call(bf16[20,256]{1,0:T(8,128)(2,1)} %sfh.1, bf16[4,256]{1,0:T(4,128)(2,1)} %tfh.1, bf16[256,2048]{1,0:T(8,128)(2,1)} %prh.1, bf16[256,2048]{1,0:T(8,128)(2,1)} %tph.1, s32[5,128]{1,0:T(8,128)} %bitcast.3, s32[2,640]{1,0:T(2,128)} %bitcast.2), custom_call_target="tpu_custom_call" | custom-call | tf_op jit(solution)/shard_map/pallas_call | solution.py:435
  59.4 1.7 %shard_map.78 = (f32[20,256]{1,0:T(8,128)}, f32[32,2048]{1,0:T(8,128)}) custom-call(f32[20,256]{1,0:T(8,128)} %get-tuple-element.4.student, f32[32,2048]{1,0:T(8,128)} %get-tuple-element.5.proto), custom_call_target="tpu_custom_call" | custom-call | tf_op jit(solution)/shard_map/pallas_call | solution.py:499

commit v2 on v1

--- a/solution.py
+++ b/solution.py
@@ -177,6 +177,44 @@
         pnorm[:, cols] = n
         wb[:, cols] = (v * (1.0 / n)).astype(BF16)
 
+    arrived(X_TEACH, "proto", teach)
+    for p in range(NPR):
+        v = teach[p]
+        x32[4 * p : 4 * p + 4, 0:128] = v[0:4]
+        x32[4 * p : 4 * p + 4, 128:256] = v[4:8]
+    tgrp[dp] = x32[0:T, :].astype(BF16)
+
+    def assign(g):
+        rows = tgrp[g]
+        for j in range(C // CH):
+            e = jnp.exp(dot(rows, tpb[:, CH * j : CH * j + CH]) * TEACHER_SCALE)
+            ass[group_rows(g), CH * j : CH * j + CH] = e
+
+    assign(dp)
+
+    def column_part(g, acc, arow, table=ass):
+        if arow is not None:
+            wide = row_to_columns(arow)
+        for i in range(T // 8):
+            e = table[pl.ds(pl.multiple_of(g * T + 8 * i, 8), 8), :]
+            if arow is not None:
+                e = e * jnp.concatenate([wide[8 * i : 8 * i + 8]] * (C // 128), axis=1)
+            acc = acc + e
+        return acc
+
+    def row_part(g):
+        cb = jnp.broadcast_to(cvec[...], (8, C))
+        parts = []
+        for i in range(T // 8):
+            parts.append(lane_tiles(ass[pl.ds(pl.multiple_of(g * T + 8 * i, 8), 8), :] * cb))
+        return columns_to_row(jnp.concatenate(parts, axis=0))
+
+    col1[dp] = jnp.sum(column_part(dp, jnp.zeros((8, C), F32), None), axis=0, keepdims=True)
+    send(X_COL1, "dp", col1)
+    send(X_TGRP, "dp", tgrp)
+    arrived(X_STUDZ, "z", stud.at[py])
+    send(X_STUDY, "y", stud)
+
     loads[4].wait()
     loads[5].wait()
     lanes = lax.broadcasted_iota(jnp.int32, (128, 128), 1).astype(F32)
@@ -190,44 +228,6 @@
         scalec[128 * i : 128 * i + 128, :] = w0 + w1
     own_rows = lax.broadcasted_iota(jnp.int32, (32, R), 0) + pi * OWN
     ownsel[...] = (lax.broadcasted_iota(jnp.int32, (32, R), 1) == own_rows).astype(F32)
-
-    arrived(X_TEACH, "proto", teach)
-    for p in range(NPR):
-        v = teach[p]
-        x32[4 * p : 4 * p + 4, 0:128] = v[0:4]
-        x32[4 * p : 4 * p + 4, 128:256] = v[4:8]
-    tgrp[dp] = x32[0:T, :].astype(BF16)
-
-    def assign(g):
-        rows = tgrp[g]
-        for j in range(C // CH):
-            e = jnp.exp(dot(rows, tpb[:, CH * j : CH * j + CH]) * TEACHER_SCALE)
-            ass[group_rows(g), CH * j : CH * j + CH] = e
-
-    assign(dp)
-
-    def column_part(g, acc, arow, table=ass):
-        if arow is not None:
-            wide = row_to_columns(arow)
-        for i in range(T // 8):
-            e = table[pl.ds(pl.multiple_of(g * T + 8 * i, 8), 8), :]
-            if arow is not None:
-                e = e * jnp.concatenate([wide[8 * i : 8 * i + 8]] * (C // 128), axis=1)
-            acc = acc + e
-        return acc
-
-    def row_part(g):
-        cb = jnp.broadcast_to(cvec[...], (8, C))
-        parts = []
-        for i in range(T // 8):
-            parts.append(lane_tiles(ass[pl.ds(pl.multiple_of(g * T + 8 * i, 8), 8), :] * cb))
-        return columns_to_row(jnp.concatenate(parts, axis=0))
-
-    col1[dp] = jnp.sum(column_part(dp, jnp.zeros((8, C), F32), None), axis=0, keepdims=True)
-    send(X_COL1, "dp", col1)
-    send(X_TGRP, "dp", tgrp)
-    arrived(X_STUDZ, "z", stud.at[py])
-    send(X_STUDY, "y", stud)
 
     arrived(X_COL1, "dp", col1)
     cvec[...] = 1.0 / jnp.sum(col1[...], axis=0)

time: 61.2 us -> 61.2 us (level)
  no operation moved by 1% of the time
where the time goes in v2:
time: 61.2 us; the launch traced here: 61.1 us
  Pallas kernels  60.4 us (99%)
  between operations  0.64 us (1%)
    pallas_call x1, Pallas kernels, per_device(): pl.pallas_call(kernel, out_shape=outs, in_specs=[anywhere] * 6, out_specs...  58.7 us
    pallas_call x1, Pallas kernels, per_device(): pl.pallas_call(last_step, out_shape=outs, in_specs=[vmem] * 2, out_specs=...  1.69 us

profile of v2, /device:TPU:1, one launch (start us, length us, event | category | flops | bytes accessed | tf_op | source)
XLA Modules:
  0.0 61.1 jit_solution(14663753120666663703)
XLA Ops:
  0.6 58.7 %shard_map.77 = (f32[20,256]{1,0:T(8,128)}, f32[32,2048]{1,0:T(8,128)}) custom-call(bf16[20,256]{1,0:T(8,128)(2,1)} %sfh.1, bf16[4,256]{1,0:T(4,128)(2,1)} %tfh.1, bf16[256,2048]{1,0:T(8,128)(2,1)} %prh.1, bf16[256,2048]{1,0:T(8,128)(2,1)} %tph.1, s32[5,128]{1,0:T(8,128)} %bitcast.3, s32[2,640]{1,0:T(2,128)} %bitcast.2), custom_call_target="tpu_custom_call" | custom-call | tf_op jit(solution)/shard_map/pallas_call | solution.py:435
  59.4 1.7 %shard_map.78 = (f32[20,256]{1,0:T(8,128)}, f32[32,2048]{1,0:T(8,128)}) custom-call(f32[20,256]{1,0:T(8,128)} %get-tuple-element.4.student, f32[32,2048]{1,0:T(8,128)} %get-tuple-element.5.proto), custom_call_target="tpu_custom_call" | custom-call | tf_op jit(solution)/shard_map/pallas_call | solution.py:499
